TPU v7x, 512 devices: a whole 4x4x16 slice. The times are simulated.
512 devices in a mesh: wide: 32 (over z, core), narrow: 16 (over x, y).
Axes of the slice: x: 4, y: 4, z: 16, core: 2. Of those that a mesh axis runs over, the one named last changes fastest.
Arguments:
- coded: bfloat16 [1024, 98304], P('narrow', 'wide'), may hold values from -0.5 to 1.5
- exponents: int32 [32, 98304], P('narrow', 'wide'), may hold values from -2 to 2
- boot_counts: int32 [16, 98304], P(None, 'wide'), may hold values from 0 to 8
- tile_rows: int32 [32], replicated, may hold values from 0 to 31, each once
Outputs:
- owned: float32 [16, 1024, 1024], P(None, 'wide', 'narrow')
Inputs may be any that keep to these rules, and one draw needn't show every extreme that they name: tile_rows holds each of 0 to 31 once.
All inputs are finite; a program needn't handle non-finite values.
Results may differ from a plain program's by a relative error of at most 0.0003.
Values may be sent and summed in bfloat16 or wider, within the bound.
A program may use at most 64 MiB of HBM per device.

v0:
```python
import jax
import jax.numpy as jnp
from jax import lax
from jax.sharding import PartitionSpec as P

QB = 32


def decode(coded, exponents, block_width):
    scale = jnp.repeat(jnp.exp2(exponents.astype(jnp.float32)), block_width, axis=0)
    return (coded.astype(jnp.float32) * scale).astype(jnp.bfloat16)


def weigh(features, boot_counts):
    count_rows = boot_counts.astype(jnp.float32)
    stacked = features.astype(jnp.float32)[None, :, :] * count_rows[:, None, :]
    return stacked.astype(jnp.bfloat16).reshape(-1, features.shape[1])


def per_device(coded, exponents, boot_counts, tile_rows):
    col_count, row_count = coded.shape
    replicas = boot_counts.shape[0]
    features = decode(coded, exponents, QB)
    weighted = weigh(features, boot_counts)
    width = col_count * lax.axis_size("narrow")
    tiles = lax.axis_size("wide")
    tile_size = width // tiles
    total = row_count * tiles
    partial_value = lax.dot_general(
        lax.all_gather(features, "narrow", axis=0, tiled=True),
        weighted,
        (((1,), (1,)), ((), ())),
        preferred_element_type=jnp.float32,
    )
    blocks = partial_value.reshape(tiles, tile_size, replicas * col_count)
    summed = lax.psum_scatter(
        jnp.take(blocks, tile_rows, axis=0).reshape(width, replicas * col_count),
        "wide",
        scatter_dimension=0,
        tiled=True,
    )
    mine = tile_rows[lax.axis_index("wide")]
    gram_rows = mine * tile_size + jnp.arange(tile_size, dtype=jnp.int32)
    gram_cols = lax.axis_index("narrow") * col_count + jnp.arange(col_count, dtype=jnp.int32)
    keep = gram_cols[None, :] <= gram_rows[:, None]
    result = summed.reshape(tile_size, replicas, col_count) / total
    result = jnp.where(keep[:, None, :], result, 0.0)
    return result.transpose(1, 0, 2)


def solution(mesh):
    placed = (P("narrow", "wide"), P("narrow", "wide"), P(None, "wide"), P())
    return jax.shard_map(
        per_device, mesh=mesh, in_specs=placed, out_specs=P(None, "wide", "narrow"), check_vma=False
    )
```

profile of v0, /device:TPU:1, one launch (start us, length us, event | category | flops | bytes accessed | tf_op | source)
XLA Modules:
  0.0 233.3 jit_solution(9596444817346966437)
XLA Ops:
  6.5 0.0 all-gather.2.cloned.1.call-start
  6.5 0.8 multiply_exponential_fusion
  7.3 1.9 fusion.1
  9.2 0.0 all-gather.2.cloned.1.call-update
  9.2 0.0 reduce-scatter.2.cloned.1.call-start
  9.2 0.9 convert_element_type.32
  10.2 0.7 compare_and_fusion
  10.9 0.1 broadcast_in_dim.37
  10.9 0.1 broadcast_in_dim.38
  11.0 0.7 compare_select_fusion
  11.7 4.1 %multiply_convert_fusion = bf16[16,64,3072]{2,1,0:T(8,128)(2,1)} fusion(f32[16,3072]{1,0:T(8,128)S(1)} %convert_element_type.32, f32[64,3072]{1,0:T(8,128)S(1)} %get-tuple-element.5), kind=kLoop, calls=%fused_computation.1 | loop fusion | flops 6291456 | bytes 7274496 | tf_op jit(solution)/shard_map/convert_element_type | solution.py:17
  15.8 76.6 %all-gather.2.cloned.1.call-done = bf16[1024,3072]{1,0:T(8,128)(2,1)} async-done(((bf16[64,3072]{1,0:T(8,128)(2,1)}), bf16[1024,3072]{1,0:T(8,128)(2,1)}) %all-gather.2.cloned.1.call-update) | async-done | bytes 6291472 | tf_op jit(solution)/shard_map/all_gather | solution.py:30
  92.4 12.0 %fusion.3 = f32[32,32,1024]{2,1,0:T(8,128)} fusion(bf16[32,32,3072]{2,1,0:T(8,128)(2,1)} %bitcast.17, bf16[1024,3072,1]{1,0,2:T(8,128)(2,1)} %bitcast.16), kind=kOutput, calls=%fused_computation.15 | convolution fusion | flops 6442450944 | bytes 16777216 | tf_op jit(solution)/shard_map/dot_general | solution.py:29
  104.4 4.9 %gather_fusion = f32[32,32,1024]{2,1,0:T(8,128)} fusion(f32[32,32,1024]{2,1,0:T(8,128)} %fusion.3, s32[1024]{0:T(1024)S(1)} %pad_clamp_fusion), kind=kCustom, calls=%fused_computation | custom fusion | bytes 8388736 | tf_op jit(solution)/shard_map/jit(_take)/gather | solution.py:37
  109.3 0.0 copy-start
  109.3 4.5 %bitcast_select_fusion = f32[1024,1024]{1,0:T(8,128)} fusion(f32[32,32,1024]{2,1,0:T(8,128)} %gather_fusion, pred[1024]{0:T(1024)(128)(4,1)S(1)} %broadcast_in_dim.38), kind=kLoop, calls=%fused_computation.2 | loop fusion | flops 1048576 | bytes 8389632 | tf_op jit(solution)/shard_map/jit(_take)/select_n | solution.py:37
  113.9 0.0 reduce-scatter.2.cloned.1.call-update
  113.9 0.0 copy-done
  113.9 0.6 dynamic_slice.3
  115.2 0.1 broadcast_compare_fusion
  115.2 109.4 %reduce-scatter.2.cloned.1.call-done = f32[32,1024]{1,0:T(8,128)} async-done(((f32[1024,1024]{1,0:T(8,128)}), f32[32,1024]{1,0:T(8,128)}) %reduce-scatter.2.cloned.1.call-update) | async-done | bytes 131088 | tf_op jit(solution)/shard_map/reduce_scatter | solution.py:36
  224.6 0.9 broadcast_multiply_fusion
  225.5 0.1 div.10
  225.7 0.8 copy.5
  (4 shorter events, 0.0 us)
Async XLA Ops:
  6.5 85.9 %all-gather.2.cloned.1.call-start = ((), (), s32[]{:S(2)}) async-start(), calls=%async_computation.1 | async-start | bytes 6684672 | tf_op jit(solution)/shard_map/all_gather | solution.py:30
  9.2 215.4 %reduce-scatter.2.cloned.1.call-start = ((), (), s32[]{:S(2)}) async-start(), calls=%async_computation.2 | async-start | bytes 4325376 | tf_op jit(solution)/shard_map/reduce_scatter | solution.py:36
  109.3 4.6 %copy-start = (s32[32]{0:T(128)S(1)}, s32[32]{0:T(128)}, u32[]{:S(2)}) copy-start(s32[32]{0:T(128)} %param.7) | copy-start | bytes 388
Sparse Core Ops, SparseCore 0:
  10.4 81.9 all-gather.1
  114.0 110.5 reduce-scatter.1
where the time goes:
time: 236 us; the launch traced here: 233 us
  waiting for transfers between devices  186 us (79%)
  other arithmetic  14.6 us (6%)
  between operations  14.1 us (6%)
  matrix products  12 us (5%)
  local copies, waits for them, and re-layouts  6.58 us (3%)
    reduce_scatter x1, waiting for transfers between devices, per_device(): lax.psum_scatter(jnp.take(blocks, tile_rows, axis=0).reshape(width, repli...  109 us
    all_gather x1, waiting for transfers between devices, per_device(): lax.all_gather(features, 'narrow', axis=0, tiled=True)  76.6 us
    dot_general x1, matrix products, per_device(): lax.dot_general(lax.all_gather(features, 'narrow', axis=0, tiled=True), w...  12 us
    select_n x2, other arithmetic, per_device(): jnp.take(blocks, tile_rows, axis=0).reshape(width, replicas * col_count)  5.19 us
    gather x1, local copies, waits for them, and re-layouts, per_device(): jnp.take(blocks, tile_rows, axis=0).reshape(width, replicas * col_count)  4.93 us
  transfers between devices with their start and end apart: 2, of which 2 were waited for; matrix products, arithmetic and copies ran while one was open for 3% of the time, Pallas kernels for 0%

commit v1 on v0

v1 whole, which is shorter than its diff:
```python
import jax
import jax.numpy as jnp
from jax import lax
from jax.experimental import pallas as pl
from jax.experimental.pallas import tpu as pltpu
from jax.sharding import PartitionSpec as P

MESH = pl.DeviceIdType.MESH
QB = 32
SIDE = 4
NZ = 16
WIDE = 32
COLS = 64
HALF = 32
REPLICAS = 16
TOTAL = 98304
CHUNKS = 4
F32 = jnp.float32
BF16 = jnp.bfloat16


def remote(src, dst, send_sem, recv_sem, wide, narrow):
    return pltpu.make_async_remote_copy(
        src_ref=src, dst_ref=dst, send_sem=send_sem, recv_sem=recv_sem,
        device_id={"wide": wide, "narrow": narrow}, device_id_type=MESH,
    )


def scale_exponent(largest):
    return jnp.ceil(jnp.log2(jnp.maximum(largest, 1e-30)))


def to_int16(values, factor):
    scaled = jnp.floor(values * factor + 0.5)
    return jnp.clip(scaled, -32767.0, 32767.0).astype(jnp.int32).astype(jnp.int16)


def from_int16(values, factor):
    return values.astype(jnp.int32).astype(F32) * factor


def put_coded(dst, index, parts):
    largest = jnp.max(jnp.abs(parts[0]), axis=0, keepdims=True)
    for part in parts[1:]:
        largest = jnp.maximum(largest, jnp.max(jnp.abs(part), axis=0, keepdims=True))
    exponent = scale_exponent(largest)
    factor = jnp.exp2(15.0 - exponent)
    for place, part in enumerate(parts):
        dst[(*index, pl.ds(64 * place, 64))] = to_int16(part, factor)
    tile = jnp.broadcast_to(exponent, (16, 128)).astype(jnp.int32).astype(jnp.int16)
    dst[(*index, pl.ds(64 * len(parts), 16))] = tile


def get_coded(src, index, place, count):
    tile = src[(*index, pl.ds(64 * count, 16))].astype(jnp.int32).astype(F32)
    factor = jnp.exp2(tile[0:1] - 15.0)
    return from_int16(src[(*index, pl.ds(64 * place, 64))], factor)


def kernel(coded, exponents, counts, tile_rows, out,
           xl, yl, cb, w1, w2, acc1, acc2, peer1, peer2, u, q1, near, far, u2, q2, last, f_buf,
           g_buf, r_buf, tiles, send_tiles, got,
           gs, gr, ps, pr, s1s, s1r, s2s, s2r, x1s, x1r, x2s, x2r):
    w = lax.axis_index("wide")
    n = lax.axis_index("narrow")
    z, c = w // 2, w % 2
    x, y = n // SIDE, n % SIDE
    k_all = coded.shape[1]
    kc_len = k_all // CHUNKS

    def at(x_, y_):
        return lax.rem(x_ + SIDE, SIDE) * SIDE + lax.rem(y_ + SIDE, SIDE)

    def zc(z_, c_):
        return lax.rem(z_ + NZ, NZ) * 2 + c_

    barrier = pltpu.get_barrier_semaphore()
    for d in range(1, SIDE):
        for narrow in (at(x + d, y), at(x, y + d)):
            pl.semaphore_signal(barrier, inc=1, device_id={"wide": w, "narrow": narrow}, device_id_type=MESH)

    def greet(d, carry):
        pl.semaphore_signal(barrier, inc=1, device_id={"wide": lax.rem(w + d, WIDE), "narrow": n}, device_id_type=MESH)
        return carry

    lax.fori_loop(1, WIDE, greet, 0)

    for kc in range(CHUNKS):
        cols = pl.ds(kc * kc_len, kc_len)
        for half in range(2):
            scale = jnp.exp2(exponents[half:half + 1, cols].astype(F32))
            rows = pl.ds(half * QB, QB)
            block = (coded[rows, cols].astype(F32) * scale).astype(BF16)
            xl[kc, y, rows, :] = block
            yl[kc, x, rows, :] = block
        for r in range(REPLICAS):
            row = counts[r:r + 1, cols].astype(F32)
            cb[kc, r] = jnp.broadcast_to(row, (16, kc_len)).astype(BF16)

    pl.semaphore_wait(barrier, 2 * (SIDE - 1) + WIDE - 1)

    def own_copies(kc):
        src = xl.at[kc, y]
        return [
            remote(src, xl.at[kc, y], gs.at[kc, 0], gr.at[kc, 0], w, at(x, y + 1)),
            remote(src, xl.at[kc, y], gs.at[kc, 1], gr.at[kc, 1], w, at(x, y - 1)),
            remote(src, yl.at[kc, x], gs.at[kc, 2], gr.at[kc, 2], w, at(x + 1, y)),
            remote(src, yl.at[kc, x], gs.at[kc, 3], gr.at[kc, 3], w, at(x - 1, y)),
        ]

    def wrap(v):
        return lax.rem(v + SIDE, SIDE)

    lo, hi = pl.ds(0, HALF), pl.ds(HALF, HALF)

    def forward_copies(kc):
        ym, yp, xm, xp = wrap(y - 1), wrap(y + 1), wrap(x - 1), wrap(x + 1)
        return [
            remote(xl.at[kc, ym, lo], xl.at[kc, ym, lo], gs.at[kc, 4], gr.at[kc, 4], w, at(x, y + 1)),
            remote(xl.at[kc, yp, hi], xl.at[kc, yp, hi], gs.at[kc, 5], gr.at[kc, 5], w, at(x, y - 1)),
            remote(yl.at[kc, xm, lo], yl.at[kc, xm, lo], gs.at[kc, 6], gr.at[kc, 6], w, at(x + 1, y)),
            remote(yl.at[kc, xp, hi], yl.at[kc, xp, hi], gs.at[kc, 7], gr.at[kc, 7], w, at(x - 1, y)),
        ]

    def wait_near(kc):
        places = [xl.at[kc, wrap(y - 1)], xl.at[kc, wrap(y + 1)], yl.at[kc, wrap(x - 1)], yl.at[kc, wrap(x + 1)]]
        for i, place in enumerate(places):
            remote(place, place, gs.at[kc, i], gr.at[kc, i], w, at(x, y + 1)).wait_recv()

    def wait_far(kc):
        yo, xo = wrap(y + 2), wrap(x + 2)
        places = [xl.at[kc, yo, lo], xl.at[kc, yo, hi], yl.at[kc, xo, lo], yl.at[kc, xo, hi]]
        for i, place in enumerate(places):
            remote(place, place, gs.at[kc, 4 + i], gr.at[kc, 4 + i], w, at(x, y + 1)).wait_recv()

    dims = (((1,), (1,)), ((), ()))

    def compute(kc):
        x_all = xl[kc].reshape(SIDE * COLS, kc_len)
        y_all = yl[kc].reshape(SIDE * COLS, kc_len)

        def first(rp, carry):
            for k in range(2):
                count = cb[kc, 2 * rp + k]
                for y1 in range(SIDE):
                    for part in range(2):
                        feats = xl[kc, y1, 16 * part:16 * part + 16, :]
                        w1[pl.ds(128 * k + HALF * y1 + 16 * part, 16), :] = feats * count
            res = lax.dot_general(y_all, w1[...], dims, preferred_element_type=F32)
            if kc == 0:
                acc1[rp] = res
            else:
                acc1[rp] += res
            return carry

        lax.fori_loop(0, REPLICAS // 2, first, 0)

        for x1 in range(SIDE):
            @pl.when(x1 <= x)
            def _():
                for r in range(REPLICAS):
                    count = cb[kc, r]
                    for part in range(2):
                        feats = yl[kc, x1, HALF + 16 * part:HALF + 16 * part + 16, :]
                        w2[pl.ds(HALF * r + 16 * part, 16), :] = feats * count
                res = lax.dot_general(w2[...], x_all, dims, preferred_element_type=F32)
                if kc == 0:
                    acc2[x1] = res
                else:
                    acc2[x1] += res

    for kc in range(min(2, CHUNKS)):
        for copy in own_copies(kc):
            copy.start()
    for kc in range(CHUNKS):
        wait_near(kc)
        for copy in forward_copies(kc):
            copy.start()
        if kc + 2 < CHUNKS:
            for copy in own_copies(kc + 2):
                copy.start()
        if kc >= 1:
            wait_far(kc - 1)
            compute(kc - 1)
    wait_far(CHUNKS - 1)
    compute(CHUNKS - 1)

    other = zc(z, 1 - c)

    def peer_copy(kind, s):
        if kind == 0:
            place = (slice(None), pl.ds(64 * s, 64))
            return remote(acc1.at[place], peer1.at[place], ps.at[s], pr.at[s], other, n)
        return remote(acc2.at[s], peer2.at[s], ps.at[s], pr.at[s], other, n)

    def used(kind, s):
        return (s >= x) if kind == 0 else (s <= x)

    for kind in range(2):
        for s in range(SIDE):
            @pl.when(jnp.logical_and(c == 1 - kind, used(kind, s)))
            def _():
                peer_copy(kind, s).start()

    for kind in range(2):
        for s in range(SIDE):
            @pl.when(jnp.logical_and(c == kind, used(kind, s)))
            def _():
                peer_copy(kind, s).wait_recv()
                for r in range(REPLICAS):
                    if kind == 0:
                        place = (r // 2, pl.ds(64 * s, 64), pl.ds(128 * (r % 2), 128))
                        u[s, r % 4, r // 4] = acc1[place] + peer1[place]
                    else:
                        for half in range(2):
                            place = (s, pl.ds(HALF * r, HALF), pl.ds(128 * half, 128))
                            u[s, r % 4, r // 4, 32 * half:32 * half + 32, :] = acc2[place] + peer2[place]

    def live(s):
        return jnp.logical_or(jnp.logical_and(c == 0, s >= x), jnp.logical_and(c == 1, s <= x))

    cls = lax.rem(z, 4)

    def klass(d):
        return lax.rem(cls + d + 4, 4)

    def near_copies(s):
        return [
            remote(q1.at[s, klass(1)], near.at[0, s], s1s.at[0, s], s1r.at[0, s], zc(z + 1, c), n),
            remote(q1.at[s, klass(-1)], near.at[1, s], s1s.at[1, s], s1r.at[1, s], zc(z - 1, c), n),
            remote(q1.at[s, klass(2), 0], far.at[0, s], s1s.at[2, s], s1r.at[2, s], zc(z + 2, c), n),
            remote(q1.at[s, klass(2), 1], far.at[1, s], s1s.at[3, s], s1r.at[3, s], zc(z - 2, c), n),
        ]

    for s in range(SIDE):
        @pl.when(live(s))
        def _():
            copies = near_copies(s)
            for d, parts in ((2, copies[2:]), (1, copies[:1]), (-1, copies[1:2])):
                for half in range(2):
                    put_coded(q1, (s, klass(d), half), [u[s, klass(d), 2 * half], u[s, klass(d), 2 * half + 1]])
                for copy in parts:
                    copy.start()

    step = z // 4

    def hop_copy(s, d):
        i = lax.rem(step + d, 4)
        return remote(q2.at[s, i], last.at[d - 1, s], s2s.at[d - 1, s], s2r.at[d - 1, s], zc(cls + 4 * i, c), n)

    for s in range(SIDE):
        @pl.when(live(s))
        def _():
            for copy in near_copies(s):
                copy.wait_recv()
            for half in range(2):
                for place in range(2):
                    i = 2 * half + place
                    u2[s, i] = (
                        (u[s, cls, i] + get_coded(near, (0, s, half), place, 2))
                        + (get_coded(near, (1, s, half), place, 2) + get_coded(far, (half, s), place, 2))
                    )
            for d in (2, 1, 3):
                i = lax.rem(step + d, 4)
                put_coded(q2, (s, i), [u2[s, i]])
                hop_copy(s, d).start()

    for s in range(SIDE):
        @pl.when(live(s))
        def _():
            total = u2[s, step]
            for d in (1, 2, 3):
                hop_copy(s, d).wait_recv()
                total = total + get_coded(last, (d - 1, s), 0, 1)
            f_buf[s] = total

        @pl.when(jnp.logical_not(live(s)))
        def _():
            f_buf[s] = jnp.zeros((64, 128), F32)

    @pl.when(c == 0)
    def _():
        for y1 in range(SIDE):
            g_buf[y1] = jnp.concatenate([f_buf[x1, :, HALF * y1:HALF * y1 + HALF] for x1 in range(SIDE)], axis=1)

    @pl.when(c == 1)
    def _():
        for x1 in range(SIDE):
            turned = [f_buf[x1, HALF * half:HALF * half + HALF, :].T for half in range(2)]
            g_buf[x1] = jnp.concatenate([turned[y1 // 2][64 * (y1 % 2):64 * (y1 % 2) + 64] for y1 in range(SIDE)], axis=1)

    place = jnp.where(c == 0, y, x)

    def line_copy(d):
        to = lax.rem(place + d, SIDE)
        narrow = jnp.where(c == 0, at(x, to), at(to, y))
        return remote(g_buf.at[to], r_buf.at[place], x1s.at[d - 1], x1r.at[d - 1], w, narrow)

    for d in (2, 1, 3):
        line_copy(d).start()
    r_buf[place] = g_buf[place]
    for d in range(1, SIDE):
        spot = r_buf.at[lax.rem(place - d + SIDE, SIDE)]
        remote(spot, spot, x1s.at[d - 1], x1r.at[d - 1], w, n).wait_recv()

    sub = lax.broadcasted_iota(jnp.int32, (8, 128), 0)
    lane = lax.broadcasted_iota(jnp.int32, (8, 128), 1)
    offset = sub + 8 * (lane // HALF) - lane % HALF - COLS * n - HALF * c
    for q in range(SIDE):
        for hh in range(2):
            groups = [r_buf[q, 32 * hh + 8 * k:32 * hh + 8 * k + 8, :] for k in range(4)]
            for g in range(SIDE):
                t = 2 * jnp.where(c == 0, SIDE * g + q, SIDE * q + g) + hh
                tile = jnp.concatenate([group[:, HALF * g:HALF * g + HALF] for group in groups], axis=1)
                tiles[t] = jnp.where(offset + 32 * t >= 0, tile / TOTAL, 0.0)

    def pick(j, carry):
        send_tiles[j] = tiles[tile_rows[j]]
        return carry

    lax.fori_loop(0, WIDE, pick, 0)

    def tile_copy(d):
        j = lax.rem(w + d, WIDE)
        return remote(send_tiles.at[j], got.at[w], x2s, x2r, j, n)

    def send_one(d, carry):
        tile_copy(d).start()
        return carry

    lax.fori_loop(1, WIDE, send_one, 0)
    got[w] = send_tiles[w]

    for kc in range(CHUNKS):
        for copy in own_copies(kc) + forward_copies(kc):
            copy.wait_send()
    for kind in range(2):
        for s in range(SIDE):
            @pl.when(jnp.logical_and(c == 1 - kind, used(kind, s)))
            def _():
                peer_copy(kind, s).wait_send()
    for s in range(SIDE):
        @pl.when(live(s))
        def _():
            for copy in near_copies(s):
                copy.wait_send()
            for d in (1, 2, 3):
                hop_copy(s, d).wait_send()
    for d in range(1, SIDE):
        line_copy(d).wait_send()

    most = pl.ds(0, WIDE - 1)
    every = remote(send_tiles.at[most], got.at[most], x2s, x2r, w, n)
    every.wait_recv()
    for r in range(REPLICAS):
        both = [got[2 * r], got[2 * r + 1]]
        for k in range(4):
            out[r, 8 * k:8 * k + 8, :] = jnp.concatenate(
                [part[:, HALF * k:HALF * k + HALF] for part in both], axis=1)
    every.wait_send()


def per_device(coded, exponents, boot_counts, tile_rows):
    k_all = coded.shape[1]
    kc_len = k_all // CHUNKS
    vmem = pl.BlockSpec(memory_space=pltpu.VMEM)
    dma = pltpu.SemaphoreType.DMA
    i16 = jnp.int16
    scratch = [
        pltpu.VMEM((CHUNKS, SIDE, COLS, kc_len), BF16),
        pltpu.VMEM((CHUNKS, SIDE, COLS, kc_len), BF16),
        pltpu.VMEM((CHUNKS, REPLICAS, 16, kc_len), BF16),
        pltpu.VMEM((256, kc_len), BF16),
        pltpu.VMEM((HALF * REPLICAS, kc_len), BF16),
        pltpu.VMEM((REPLICAS // 2, 256, 256), F32),
        pltpu.VMEM((SIDE, HALF * REPLICAS, 256), F32),
        pltpu.VMEM((REPLICAS // 2, 256, 256), F32),
        pltpu.VMEM((SIDE, HALF * REPLICAS, 256), F32),
        pltpu.VMEM((SIDE, 4, 4, 64, 128), F32),
        pltpu.VMEM((SIDE, 4, 2, 144, 128), i16),
        pltpu.VMEM((2, SIDE, 2, 144, 128), i16),
        pltpu.VMEM((2, SIDE, 144, 128), i16),
        pltpu.VMEM((SIDE, 4, 64, 128), F32),
        pltpu.VMEM((SIDE, 4, 80, 128), i16),
        pltpu.VMEM((3, SIDE, 80, 128), i16),
        pltpu.VMEM((SIDE, 64, 128), F32),
        pltpu.VMEM((SIDE, 64, 128), F32),
        pltpu.VMEM((SIDE, 64, 128), F32),
        pltpu.VMEM((WIDE, 8, 128), F32),
        pltpu.VMEM((WIDE, 8, 128), F32),
        pltpu.VMEM((WIDE, 8, 128), F32),
        dma((CHUNKS, 8)), dma((CHUNKS, 8)),
        dma((SIDE,)), dma((SIDE,)),
        dma((4, SIDE)), dma((4, SIDE)),
        dma((3, SIDE)), dma((3, SIDE)),
        dma((3,)), dma((3,)),
        dma, dma,
    ]
    return pl.pallas_call(
        kernel,
        out_shape=jax.ShapeDtypeStruct((REPLICAS, 32, COLS), F32),
        in_specs=[vmem, vmem, vmem, pl.BlockSpec(memory_space=pltpu.SMEM)],
        out_specs=vmem,
        scratch_shapes=scratch,
        compiler_params=pltpu.CompilerParams(
            collective_id=0, has_side_effects=True, vmem_limit_bytes=48 * 1024 * 1024),
        cost_estimate=pl.CostEstimate(flops=2 * 1024 * 1024 * k_all, bytes_accessed=2 * 1024 * 1024, transcendentals=0),
    )(coded, exponents, boot_counts, tile_rows)


def solution(mesh):
    placed = (P("narrow", "wide"), P("narrow", "wide"), P(None, "wide"), P())
    return jax.shard_map(
        per_device, mesh=mesh, in_specs=placed, out_specs=P(None, "wide", "narrow"), check_vma=False
    )
```

time: 236 us -> 88.1 us (0.37); the launches traced: 233 us -> 87.8 us
  waiting for transfers between devices: 186 us -> 0 us
  Pallas kernels: 0 us -> 83.8 us
  other arithmetic: 14.6 us -> 0 us
  between operations: 14.1 us -> 0.01 us
  matrix products: 12 us -> 0 us
  local copies, waits for them, and re-layouts: 6.58 us -> 4.02 us
    reduce_scatter x1 -> x0, waiting for transfers between devices: 109 us -> none  [per_device(): lax.psum_scatter(jnp.take(blocks, tile_rows, axis=0).reshape(width, repli...]
    pallas_call x0 -> x1, Pallas kernels: none -> 83.8 us  [per_device(): pl.pallas_call(kernel, out_shape=jax.ShapeDtypeStruct((REPLICAS, 32, COLS...]
    all_gather x1 -> x0, waiting for transfers between devices: 76.6 us -> none  [per_device(): lax.all_gather(features, 'narrow', axis=0, tiled=True)]
    dot_general x1 -> x0, matrix products: 12 us -> none  [per_device(): lax.dot_general(lax.all_gather(features, 'narrow', axis=0, tiled=True), w...]
    convert_element_type x3 -> x0, other arithmetic: 6.9 us -> none  [the longest x1 4.09 us: weigh(): return stacked.astype(jnp.bfloat16).reshape(-1, features.shape[1])]
    select_n x2 -> x0, other arithmetic: 5.19 us -> none  [per_device(): jnp.take(blocks, tile_rows, axis=0).reshape(width, replicas * col_count)]
    gather x1 -> x0, local copies, waits for them, and re-layouts: 4.93 us -> none  [per_device(): jnp.take(blocks, tile_rows, axis=0).reshape(width, replicas * col_count)]
    unnamed x2 -> x9, local copies, waits for them, and re-layouts: 0.01 us -> 4.02 us
  transfers between devices with their start and end apart: 2 -> 0, of which waited for: 2 -> 0; matrix products, arithmetic and copies ran while one was open for 3% -> 0% of each run, Pallas kernels for 0% -> 0%
where the time goes in v1:
time: 88.1 us; the launch traced here: 87.8 us
  Pallas kernels  83.8 us (95%)
  local copies, waits for them, and re-layouts  4.02 us (5%)
    pallas_call x1, Pallas kernels, per_device(): pl.pallas_call(kernel, out_shape=jax.ShapeDtypeStruct((REPLICAS, 32, COLS...  83.8 us
    unnamed x9, local copies, waits for them, and re-layouts  4.02 us

profile of v1, /device:TPU:1, one launch (start us, length us, event | category | flops | bytes accessed | tf_op | source)
XLA Modules:
  0.0 87.8 jit_solution(3979555165644501258)
XLA Ops:
  0.0 0.0 copy-start
  0.0 1.0 %copy-done = bf16[64,3072]{1,0:T(8,128)(2,1)S(1)} copy-done((bf16[64,3072]{1,0:T(8,128)(2,1)S(1)}, bf16[64,3072]{1,0:T(8,128)(2,1)}, u32[]{:S(2)}) %copy-start) | copy-done | bytes 393240
  1.0 0.0 copy-start.1
  1.0 0.9 %copy-done.1 = s32[16,3072]{1,0:T(8,128)S(1)} copy-done((s32[16,3072]{1,0:T(8,128)S(1)}, s32[16,3072]{1,0:T(8,128)}, u32[]{:S(2)}) %copy-start.1) | copy-done | bytes 196632
  1.9 0.0 copy-start.2
  1.9 0.7 copy-done.2
  2.7 0.0 copy-start.3
  2.7 0.7 copy-done.3
  3.3 83.8 %shard_map.46 = f32[16,32,64]{2,1,0:T(8,128)S(1)} custom-call(bf16[64,3072]{1,0:T(8,128)(2,1)S(1)} %copy-done, s32[2,3072]{1,0:T(2,128)S(1)} %copy-done.2, s32[16,3072]{1,0:T(8,128)S(1)} %copy-done.1, s32[32]{0:T(128)S(1)} %copy-done.3), custom_call_target="tpu_custom_call" | custom-call | flops 6442450944 | bytes 2097152 | tf_op jit(solution)/shard_map/pallas_call | solution.py:399
  87.1 0.7 copy.6
Async XLA Ops:
  0.0 1.0 %copy-start = (bf16[64,3072]{1,0:T(8,128)(2,1)S(1)}, bf16[64,3072]{1,0:T(8,128)(2,1)}, u32[]{:S(2)}) copy-start(bf16[64,3072]{1,0:T(8,128)(2,1)} %coded.1) | copy-start | bytes 1179652
  1.0 0.9 %copy-start.1 = (s32[16,3072]{1,0:T(8,128)S(1)}, s32[16,3072]{1,0:T(8,128)}, u32[]{:S(2)}) copy-start(s32[16,3072]{1,0:T(8,128)} %counts.1) | copy-start | bytes 589828
  1.9 0.7 copy-start.2
  2.7 0.7 copy-start.3

commit v2 on v1

v2 whole, which is shorter than its diff:
```python
import jax
import jax.numpy as jnp
from jax import lax
from jax.experimental import pallas as pl
from jax.experimental.pallas import tpu as pltpu
from jax.sharding import PartitionSpec as P

MESH = pl.DeviceIdType.MESH
QB = 32
SIDE = 4
NZ = 16
WIDE = 32
COLS = 64
HALF = 32
REPLICAS = 16
TOTAL = 98304
UNIT = 256
CHUNKS = ((0, 5), (5, 5), (10, 2))
F32 = jnp.float32
BF16 = jnp.bfloat16


def remote(src, dst, send_sem, recv_sem, wide, narrow):
    return pltpu.make_async_remote_copy(
        src_ref=src, dst_ref=dst, send_sem=send_sem, recv_sem=recv_sem,
        device_id={"wide": wide, "narrow": narrow}, device_id_type=MESH,
    )


def scale_exponent(largest):
    return jnp.ceil(jnp.log2(jnp.maximum(largest, 1e-30)))


def to_int16(values, factor):
    scaled = jnp.floor(values * factor + 0.5)
    return jnp.clip(scaled, -32767.0, 32767.0).astype(jnp.int32).astype(jnp.int16)


def from_int16(values, factor):
    return values.astype(jnp.int32).astype(F32) * factor


def put_coded(dst, index, parts):
    largest = jnp.max(jnp.abs(parts[0]), axis=0, keepdims=True)
    for part in parts[1:]:
        largest = jnp.maximum(largest, jnp.max(jnp.abs(part), axis=0, keepdims=True))
    exponent = scale_exponent(largest)
    factor = jnp.exp2(15.0 - exponent)
    for place, part in enumerate(parts):
        dst[(*index, pl.ds(64 * place, 64))] = to_int16(part, factor)
    tile = jnp.broadcast_to(exponent, (16, 128)).astype(jnp.int32).astype(jnp.int16)
    dst[(*index, pl.ds(64 * len(parts), 16))] = tile


def get_coded(src, index, place, count):
    tile = src[(*index, pl.ds(64 * count, 16))].astype(jnp.int32).astype(F32)
    factor = jnp.exp2(tile[0:1] - 15.0)
    return from_int16(src[(*index, pl.ds(64 * place, 64))], factor)


def kernel(coded_in, exponents_in, counts_in, tile_rows, out,
           coded, exponents, counts, xl, yl, cb, acc1, acc2, peer1, peer2, u, q1, near, far, u2, q2, last, f_buf,
           g_buf, r_buf, tiles, send_tiles, got,
           ins, gs, gr, ps, pr, s1s, s1r, s2s, s2r, x1s, x1r, x2s, x2r):
    w = lax.axis_index("wide")
    n = lax.axis_index("narrow")
    z, c = w // 2, w % 2
    x, y = n // SIDE, n % SIDE
    units = coded.shape[1] // UNIT

    def at(x_, y_):
        return lax.rem(x_ + SIDE, SIDE) * SIDE + lax.rem(y_ + SIDE, SIDE)

    def zc(z_, c_):
        return lax.rem(z_ + NZ, NZ) * 2 + c_

    inputs = [
        pltpu.make_async_copy(src, dst, ins.at[i])
        for i, (src, dst) in enumerate(((coded_in, coded), (exponents_in, exponents), (counts_in, counts)))
    ]
    for copy in inputs:
        copy.start()

    barrier = pltpu.get_barrier_semaphore()
    for narrow in (at(x + 1, y), at(x - 1, y), at(x, y + 1), at(x, y - 1)):
        pl.semaphore_signal(barrier, inc=1, device_id={"wide": w, "narrow": narrow}, device_id_type=MESH)
    for wide in (zc(z, 1 - c), zc(z + 1, c), zc(z - 1, c), zc(z + 2, c), zc(z - 2, c), zc(z + 8, c)):
        pl.semaphore_signal(barrier, inc=1, device_id={"wide": wide, "narrow": n}, device_id_type=MESH)

    for copy in inputs:
        copy.wait()
    for k in range(units):
        cols = pl.ds(k * UNIT, UNIT)
        for half in range(2):
            scale = jnp.exp2(exponents[half:half + 1, cols].astype(F32))
            rows = pl.ds(half * QB, QB)
            block = (coded[rows, cols].astype(F32) * scale).astype(BF16)
            xl[k, y, rows, :] = block
            yl[k, x, rows, :] = block
        for r in range(REPLICAS):
            row = counts[r:r + 1, cols].astype(F32)
            cb[k, r] = jnp.broadcast_to(row, (16, UNIT)).astype(BF16)

    pl.semaphore_wait(barrier, 10)

    spans = [pl.ds(*chunk) for chunk in CHUNKS]

    def own_copies(kc):
        src = xl.at[spans[kc], y]
        return [
            remote(src, xl.at[spans[kc], y], gs.at[kc, 0], gr.at[kc, 0], w, at(x, y + 1)),
            remote(src, xl.at[spans[kc], y], gs.at[kc, 1], gr.at[kc, 1], w, at(x, y - 1)),
            remote(src, yl.at[spans[kc], x], gs.at[kc, 2], gr.at[kc, 2], w, at(x + 1, y)),
            remote(src, yl.at[spans[kc], x], gs.at[kc, 3], gr.at[kc, 3], w, at(x - 1, y)),
        ]

    def wrap(v):
        return lax.rem(v + SIDE, SIDE)

    lo, hi = pl.ds(0, HALF), pl.ds(HALF, HALF)

    def forward_copies(kc):
        ym, yp, xm, xp = wrap(y - 1), wrap(y + 1), wrap(x - 1), wrap(x + 1)
        return [
            remote(xl.at[spans[kc], ym, lo], xl.at[spans[kc], ym, lo], gs.at[kc, 4], gr.at[kc, 4], w, at(x, y + 1)),
            remote(xl.at[spans[kc], yp, hi], xl.at[spans[kc], yp, hi], gs.at[kc, 5], gr.at[kc, 5], w, at(x, y - 1)),
            remote(yl.at[spans[kc], xm, lo], yl.at[spans[kc], xm, lo], gs.at[kc, 6], gr.at[kc, 6], w, at(x + 1, y)),
            remote(yl.at[spans[kc], xp, hi], yl.at[spans[kc], xp, hi], gs.at[kc, 7], gr.at[kc, 7], w, at(x - 1, y)),
        ]

    def wait_near(kc):
        places = [xl.at[spans[kc], wrap(y - 1)], xl.at[spans[kc], wrap(y + 1)], yl.at[spans[kc], wrap(x - 1)], yl.at[spans[kc], wrap(x + 1)]]
        for i, place in enumerate(places):
            remote(place, place, gs.at[kc, i], gr.at[kc, i], w, at(x, y + 1)).wait_recv()

    def wait_far(kc):
        yo, xo = wrap(y + 2), wrap(x + 2)
        places = [xl.at[spans[kc], yo, lo], xl.at[spans[kc], yo, hi], yl.at[spans[kc], xo, lo], yl.at[spans[kc], xo, hi]]
        for i, place in enumerate(places):
            remote(place, place, gs.at[kc, 4 + i], gr.at[kc, 4 + i], w, at(x, y + 1)).wait_recv()

    dims = (((1,), (1,)), ((), ()))

    def joined(pieces):
        return jnp.concatenate(pieces, axis=1)

    def parts_of(kc):
        start, count = CHUNKS[kc]
        return range(start, start + count)

    def first(kc):
        rows = joined([yl[k].reshape(SIDE * COLS, UNIT) for k in parts_of(kc)])
        feats = [xl[k, :, 0:HALF, :].reshape(8, 16, UNIT) for k in parts_of(kc)]
        for rp in range(REPLICAS // 2):
            cols = [
                joined([(f * cb[k, r][None]).reshape(128, UNIT) for f, k in zip(feats, parts_of(kc))])
                for r in (2 * rp, 2 * rp + 1)
            ]
            res = lax.dot_general(rows, jnp.concatenate(cols, axis=0), dims, preferred_element_type=F32)
            if kc == 0:
                acc1[rp] = res
            else:
                acc1[rp] += res

    def second(kc, x1):
        rows = joined([xl[k].reshape(SIDE * COLS, UNIT) for k in parts_of(kc)])
        cols = []
        for k in parts_of(kc):
            feats = yl[k, x1, HALF:COLS, :].reshape(1, 2, 16, UNIT)
            cols.append((feats * cb[k][:, None]).reshape(HALF * REPLICAS, UNIT))
        res = lax.dot_general(joined(cols), rows, dims, preferred_element_type=F32)
        if kc == 0:
            acc2[x1] = res
        else:
            acc2[x1] += res

    def second_all(kc, then=None):
        for x1 in range(SIDE):
            @pl.when(x1 <= x)
            def _():
                second(kc, x1)
                if then is not None:
                    then(x1)

    other = zc(z, 1 - c)

    def peer_copy(kind, s):
        if kind == 0:
            place = (slice(None), pl.ds(64 * s, 64))
            return remote(acc1.at[place], peer1.at[place], ps.at[s], pr.at[s], other, n)
        return remote(acc2.at[s], peer2.at[s], ps.at[s], pr.at[s], other, n)

    def used(kind, s):
        return (s >= x) if kind == 0 else (s <= x)

    def start_all(copies):
        for copy in copies:
            copy.start()

    start_all(own_copies(0))
    start_all(own_copies(1))
    wait_near(0)
    start_all(forward_copies(0))
    start_all(own_copies(2))
    wait_near(1)
    start_all(forward_copies(1))
    wait_far(0)
    first(0)
    wait_near(2)
    start_all(forward_copies(2))
    second_all(0)
    wait_far(1)
    first(1)
    second_all(1)
    wait_far(2)

    @pl.when(c == 1)
    def _():
        first(2)
        for s in range(SIDE):
            @pl.when(used(0, s))
            def _():
                peer_copy(0, s).start()

    def send_second(s):
        @pl.when(c == 0)
        def _():
            peer_copy(1, s).start()

    second_all(2, send_second)

    @pl.when(c == 0)
    def _():
        first(2)

    for kind in range(2):
        for s in range(SIDE):
            @pl.when(jnp.logical_and(c == kind, used(kind, s)))
            def _():
                peer_copy(kind, s).wait_recv()
                for r in range(REPLICAS):
                    if kind == 0:
                        place = (r // 2, pl.ds(64 * s, 64), pl.ds(128 * (r % 2), 128))
                        u[s, r % 4, r // 4] = acc1[place] + peer1[place]
                    else:
                        for half in range(2):
                            place = (s, pl.ds(HALF * r, HALF), pl.ds(128 * half, 128))
                            u[s, r % 4, r // 4, 32 * half:32 * half + 32, :] = acc2[place] + peer2[place]

    def live(s):
        return jnp.logical_or(jnp.logical_and(c == 0, s >= x), jnp.logical_and(c == 1, s <= x))

    cls = lax.rem(z, 4)

    def klass(d):
        return lax.rem(cls + d + 4, 4)

    def near_copies(s):
        return [
            remote(q1.at[s, klass(1)], near.at[0, s], s1s.at[0, s], s1r.at[0, s], zc(z + 1, c), n),
            remote(q1.at[s, klass(-1)], near.at[1, s], s1s.at[1, s], s1r.at[1, s], zc(z - 1, c), n),
            remote(q1.at[s, klass(2), 0], far.at[0, s], s1s.at[2, s], s1r.at[2, s], zc(z + 2, c), n),
            remote(q1.at[s, klass(2), 1], far.at[1, s], s1s.at[3, s], s1r.at[3, s], zc(z - 2, c), n),
        ]

    for s in range(SIDE):
        @pl.when(live(s))
        def _():
            copies = near_copies(s)
            for d, parts in ((2, copies[2:]), (1, copies[:1]), (-1, copies[1:2])):
                for half in range(2):
                    put_coded(q1, (s, klass(d), half), [u[s, klass(d), 2 * half], u[s, klass(d), 2 * half + 1]])
                for copy in parts:
                    copy.start()

    step = z // 4

    def hop_copy(s, d):
        i = lax.rem(step + d, 4)
        return remote(q2.at[s, i], last.at[d - 1, s], s2s.at[d - 1, s], s2r.at[d - 1, s], zc(cls + 4 * i, c), n)

    for s in range(SIDE):
        @pl.when(live(s))
        def _():
            for copy in near_copies(s):
                copy.wait_recv()
            for half in range(2):
                for place in range(2):
                    i = 2 * half + place
                    u2[s, i] = (
                        (u[s, cls, i] + get_coded(near, (0, s, half), place, 2))
                        + (get_coded(near, (1, s, half), place, 2) + get_coded(far, (half, s), place, 2))
                    )
            for d in (2, 1, 3):
                i = lax.rem(step + d, 4)
                put_coded(q2, (s, i), [u2[s, i]])
                hop_copy(s, d).start()

    for s in range(SIDE):
        @pl.when(live(s))
        def _():
            total = u2[s, step]
            for d in (1, 2, 3):
                hop_copy(s, d).wait_recv()
                total = total + get_coded(last, (d - 1, s), 0, 1)
            f_buf[s] = total

        @pl.when(jnp.logical_not(live(s)))
        def _():
            f_buf[s] = jnp.zeros((64, 128), F32)

    @pl.when(c == 0)
    def _():
        for y1 in range(SIDE):
            g_buf[y1] = jnp.concatenate([f_buf[x1, :, HALF * y1:HALF * y1 + HALF] for x1 in range(SIDE)], axis=1)

    @pl.when(c == 1)
    def _():
        for x1 in range(SIDE):
            turned = [f_buf[x1, HALF * half:HALF * half + HALF, :].T for half in range(2)]
            g_buf[x1] = jnp.concatenate([turned[y1 // 2][64 * (y1 % 2):64 * (y1 % 2) + 64] for y1 in range(SIDE)], axis=1)

    place = jnp.where(c == 0, y, x)

    def line_copy(d, core):
        to = lax.rem(place + d, SIDE)
        narrow = jnp.where(c == 0, at(x, to), at(to, y))
        sem = 2 * d + core
        return remote(g_buf.at[to], r_buf.at[c, place], x1s.at[sem], x1r.at[c, d], zc(z, core), narrow)

    for d in (2, 1, 3):
        for core in range(2):
            line_copy(d, core).start()
    for core in range(2):
        @pl.when(c != core)
        def _():
            line_copy(0, core).start()
    r_buf[c, place] = g_buf[place]
    for kind in range(2):
        here = y if kind == 0 else x
        for d in range(SIDE):
            def arrived():
                spot = r_buf.at[kind, lax.rem(here - d + SIDE, SIDE)]
                remote(spot, spot, x1s.at[0], x1r.at[kind, d], other, n).wait_recv()
            if d == 0:
                pl.when(c != kind)(arrived)
            else:
                arrived()

    sub = lax.broadcasted_iota(jnp.int32, (8, 128), 0)
    lane = lax.broadcasted_iota(jnp.int32, (8, 128), 1)
    for kind in range(2):
        offset = sub + 8 * (lane // HALF) - lane % HALF - COLS * n - HALF * kind
        for q in range(SIDE):
            for hh in range(2):
                groups = [r_buf[kind, q, 32 * hh + 8 * k:32 * hh + 8 * k + 8, :] for k in range(4)]
                for g in range(SIDE):
                    t = 2 * (SIDE * g + q if kind == 0 else SIDE * q + g) + hh
                    tile = jnp.concatenate([group[:, HALF * g:HALF * g + HALF] for group in groups], axis=1)
                    tiles[t, 8 * kind:8 * kind + 8, :] = jnp.where(offset + 32 * t >= 0, tile / TOTAL, 0.0)

    def tile_copy(d):
        to = lax.rem(z + d, NZ)
        return remote(send_tiles.at[to], got.at[z], x2s, x2r, zc(to, c), n)

    for d in (8, 7, 9, 6, 10, 5, 11, 4, 12, 3, 13, 2, 14, 1, 15):
        to = lax.rem(z + d, NZ)
        send_tiles[to] = tiles[tile_rows[2 * to + c]]
        tile_copy(d).start()
    got[z] = tiles[tile_rows[w]]

    for kc in range(len(CHUNKS)):
        for copy in own_copies(kc) + forward_copies(kc):
            copy.wait_send()
    for kind in range(2):
        for s in range(SIDE):
            @pl.when(jnp.logical_and(c == 1 - kind, used(kind, s)))
            def _():
                peer_copy(kind, s).wait_send()
    for s in range(SIDE):
        @pl.when(live(s))
        def _():
            for copy in near_copies(s):
                copy.wait_send()
            for d in (1, 2, 3):
                hop_copy(s, d).wait_send()
    for d in range(1, SIDE):
        for core in range(2):
            line_copy(d, core).wait_send()
    for core in range(2):
        @pl.when(c != core)
        def _():
            line_copy(0, core).wait_send()

    most = pl.ds(0, NZ - 1)
    every = remote(send_tiles.at[most], got.at[most], x2s, x2r, other, n)
    every.wait_recv()
    for r in range(REPLICAS):
        for k in range(4):
            out[r, 8 * k:8 * k + 8, :] = jnp.concatenate(
                [got[r, 8 * kind:8 * kind + 8, HALF * k:HALF * k + HALF] for kind in range(2)], axis=1)
    every.wait_send()


def per_device(coded, exponents, boot_counts, tile_rows):
    k_all = coded.shape[1]
    units = k_all // UNIT
    vmem, hbm = pl.BlockSpec(memory_space=pltpu.VMEM), pl.BlockSpec(memory_space=pl.ANY)
    dma = pltpu.SemaphoreType.DMA
    i16 = jnp.int16
    scratch = [
        pltpu.VMEM(coded.shape, BF16),
        pltpu.VMEM(exponents.shape, jnp.int32),
        pltpu.VMEM(boot_counts.shape, jnp.int32),
        pltpu.VMEM((units, SIDE, COLS, UNIT), BF16),
        pltpu.VMEM((units, SIDE, COLS, UNIT), BF16),
        pltpu.VMEM((units, REPLICAS, 16, UNIT), BF16),
        pltpu.VMEM((REPLICAS // 2, 256, 256), F32),
        pltpu.VMEM((SIDE, HALF * REPLICAS, 256), F32),
        pltpu.VMEM((REPLICAS // 2, 256, 256), F32),
        pltpu.VMEM((SIDE, HALF * REPLICAS, 256), F32),
        pltpu.VMEM((SIDE, 4, 4, 64, 128), F32),
        pltpu.VMEM((SIDE, 4, 2, 144, 128), i16),
        pltpu.VMEM((2, SIDE, 2, 144, 128), i16),
        pltpu.VMEM((2, SIDE, 144, 128), i16),
        pltpu.VMEM((SIDE, 4, 64, 128), F32),
        pltpu.VMEM((SIDE, 4, 80, 128), i16),
        pltpu.VMEM((3, SIDE, 80, 128), i16),
        pltpu.VMEM((SIDE, 64, 128), F32),
        pltpu.VMEM((SIDE, 64, 128), F32),
        pltpu.VMEM((2, SIDE, 64, 128), F32),
        pltpu.VMEM((WIDE, 16, 128), F32),
        pltpu.VMEM((NZ, 16, 128), F32),
        pltpu.VMEM((NZ, 16, 128), F32),
        dma((3,)),
        dma((len(CHUNKS), 8)), dma((len(CHUNKS), 8)),
        dma((SIDE,)), dma((SIDE,)),
        dma((4, SIDE)), dma((4, SIDE)),
        dma((3, SIDE)), dma((3, SIDE)),
        dma((2 * SIDE,)), dma((2, SIDE)),
        dma, dma,
    ]
    return pl.pallas_call(
        kernel,
        out_shape=jax.ShapeDtypeStruct((REPLICAS, 32, COLS), F32),
        in_specs=[hbm, hbm, hbm, pl.BlockSpec(memory_space=pltpu.SMEM)],
        out_specs=vmem,
        scratch_shapes=scratch,
        compiler_params=pltpu.CompilerParams(
            collective_id=0, has_side_effects=True, vmem_limit_bytes=62 * 1024 * 1024),
        cost_estimate=pl.CostEstimate(flops=2 * 1024 * 1024 * k_all, bytes_accessed=2 * 1024 * 1024, transcendentals=0),
    )(coded, exponents, boot_counts, tile_rows)


def solution(mesh):
    placed = (P("narrow", "wide"), P("narrow", "wide"), P(None, "wide"), P())
    return jax.shard_map(
        per_device, mesh=mesh, in_specs=placed, out_specs=P(None, "wide", "narrow"), check_vma=False
    )
```

time: 88.1 us -> 78.4 us (0.89)
  Pallas kernels: 83.8 us -> 76.6 us
  local copies, waits for them, and re-layouts: 4.02 us -> 1.67 us
    pallas_call x1, Pallas kernels: 83.8 us -> 76.6 us  [per_device(): pl.pallas_call(kernel, out_shape=jax.ShapeDtypeStruct((REPLICAS, 32, COLS...]
    unnamed x9 -> x1, local copies, waits for them, and re-layouts: 4.02 us -> 1.67 us
where the time goes in v2:
time: 78.4 us; the launch traced here: 78.3 us
  Pallas kernels  76.6 us (98%)
  local copies, waits for them, and re-layouts  1.67 us (2%)
    pallas_call x1, Pallas kernels, per_device(): pl.pallas_call(kernel, out_shape=jax.ShapeDtypeStruct((REPLICAS, 32, COLS...  76.6 us
    unnamed x1, local copies, waits for them, and re-layouts  1.67 us

profile of v2, /device:TPU:1, one launch (start us, length us, event | category | flops | bytes accessed | tf_op | source)
XLA Modules:
  0.0 78.3 jit_solution(4351044128317690470)
XLA Ops:
  0.0 76.6 %shard_map.46 = f32[16,32,64]{2,1,0:T(8,128)} custom-call(bf16[64,3072]{1,0:T(8,128)(2,1)} %coded_in.1, s32[2,3072]{1,0:T(2,128)} %exponents_in.1, s32[16,3072]{1,0:T(8,128)} %counts_in.1, s32[32]{0:T(128)} %tile_rows.1), custom_call_target="tpu_custom_call" | custom-call | flops 6442450944 | bytes 2097152 | tf_op jit(solution)/shard_map/pallas_call | solution.py:443
  76.6 1.7 %copy.6 = f32[16,32,64]{2,1,0:T(8,128)} copy(f32[16,32,64]{2,1,0:T(8,128)} %shard_map.46) | data formatting | bytes 262144

commit v3 on v2

--- a/solution.py
+++ b/solution.py
@@ -61,7 +61,7 @@
 def kernel(coded_in, exponents_in, counts_in, tile_rows, out,
            coded, exponents, counts, xl, yl, cb, acc1, acc2, peer1, peer2, u, q1, near, far, u2, q2, last, f_buf,
            g_buf, r_buf, tiles, send_tiles, got,
-           ins, gs, gr, ps, pr, s1s, s1r, s2s, s2r, x1s, x1r, x2s, x2r):
+           known1, known2, known4, ins, gs, gr, ps, pr, s1s, s1r, s2s, s2r, x1s, x1r, x2s, x2r):
     w = lax.axis_index("wide")
     n = lax.axis_index("narrow")
     z, c = w // 2, w % 2
@@ -78,16 +78,15 @@
         pltpu.make_async_copy(src, dst, ins.at[i])
         for i, (src, dst) in enumerate(((coded_in, coded), (exponents_in, exponents), (counts_in, counts)))
     ]
-    for copy in inputs:
-        copy.start()
-
     barrier = pltpu.get_barrier_semaphore()
     for narrow in (at(x + 1, y), at(x - 1, y), at(x, y + 1), at(x, y - 1)):
         pl.semaphore_signal(barrier, inc=1, device_id={"wide": w, "narrow": narrow}, device_id_type=MESH)
-    for wide in (zc(z, 1 - c), zc(z + 1, c), zc(z - 1, c), zc(z + 2, c), zc(z - 2, c), zc(z + 8, c)):
+    for wide in (zc(z, 1 - c), zc(z + 1, c), zc(z - 1, c)):
         pl.semaphore_signal(barrier, inc=1, device_id={"wide": wide, "narrow": n}, device_id_type=MESH)
 
     for copy in inputs:
+        copy.start()
+    for copy in inputs[:2]:
         copy.wait()
     for k in range(units):
         cols = pl.ds(k * UNIT, UNIT)
@@ -97,11 +96,12 @@
             block = (coded[rows, cols].astype(F32) * scale).astype(BF16)
             xl[k, y, rows, :] = block
             yl[k, x, rows, :] = block
-        for r in range(REPLICAS):
-            row = counts[r:r + 1, cols].astype(F32)
-            cb[k, r] = jnp.broadcast_to(row, (16, UNIT)).astype(BF16)
-
-    pl.semaphore_wait(barrier, 10)
+
+    pl.semaphore_wait(barrier, 7)
+
+    def tell(sem, d):
+        for wide in (zc(z + d, c), zc(z - d, c)):
+            pl.semaphore_signal(sem, inc=1, device_id={"wide": wide, "narrow": n}, device_id_type=MESH)
 
     spans = [pl.ds(*chunk) for chunk in CHUNKS]
 
@@ -199,15 +199,26 @@
 
     start_all(own_copies(0))
     start_all(own_copies(1))
+    tell(known1, 1)
+    inputs[2].wait()
+    for k in range(units):
+        for r in range(REPLICAS):
+            row = counts[r:r + 1, k * UNIT:(k + 1) * UNIT].astype(F32)
+            cb[k, r] = jnp.broadcast_to(row, (16, UNIT)).astype(BF16)
     wait_near(0)
     start_all(forward_copies(0))
     start_all(own_copies(2))
+    pl.semaphore_wait(known1, 2)
+    tell(known2, 2)
     wait_near(1)
     start_all(forward_copies(1))
+    pl.semaphore_wait(known2, 2)
+    tell(known4, 4)
     wait_far(0)
     first(0)
     wait_near(2)
     start_all(forward_copies(2))
+    pl.semaphore_wait(known4, 2)
     second_all(0)
     wait_far(1)
     first(1)
@@ -405,7 +416,7 @@
 def per_device(coded, exponents, boot_counts, tile_rows):
     k_all = coded.shape[1]
     units = k_all // UNIT
-    vmem, hbm = pl.BlockSpec(memory_space=pltpu.VMEM), pl.BlockSpec(memory_space=pl.ANY)
+    vmem, hbm = pl.BlockSpec(memory_space=pltpu.VMEM), pl.BlockSpec(memory_space=pltpu.HBM)
     dma = pltpu.SemaphoreType.DMA
     i16 = jnp.int16
     scratch = [
@@ -432,6 +443,7 @@
         pltpu.VMEM((WIDE, 16, 128), F32),
         pltpu.VMEM((NZ, 16, 128), F32),
         pltpu.VMEM((NZ, 16, 128), F32),
+        pltpu.SemaphoreType.REGULAR, pltpu.SemaphoreType.REGULAR, pltpu.SemaphoreType.REGULAR,
         dma((3,)),
         dma((len(CHUNKS), 8)), dma((len(CHUNKS), 8)),
         dma((SIDE,)), dma((SIDE,)),

time: 78.4 us -> 74 us (0.944)
  Pallas kernels: 76.6 us -> 72.2 us
    pallas_call x1, Pallas kernels: 76.6 us -> 72.2 us  [per_device(): pl.pallas_call(kernel, out_shape=jax.ShapeDtypeStruct((REPLICAS, 32, COLS...]
where the time goes in v3:
time: 74 us; the launch traced here: 73.8 us
  Pallas kernels  72.2 us (98%)
  local copies, waits for them, and re-layouts  1.67 us (2%)
    pallas_call x1, Pallas kernels, per_device(): pl.pallas_call(kernel, out_shape=jax.ShapeDtypeStruct((REPLICAS, 32, COLS...  72.2 us
    unnamed x1, local copies, waits for them, and re-layouts  1.67 us

profile of v3, /device:TPU:1, one launch (start us, length us, event | category | flops | bytes accessed | tf_op | source)
XLA Modules:
  0.0 73.8 jit_solution(12972454813858633350)
XLA Ops:
  0.0 72.2 %shard_map.46 = f32[16,32,64]{2,1,0:T(8,128)} custom-call(bf16[64,3072]{1,0:T(8,128)(2,1)} %coded_in.1, s32[2,3072]{1,0:T(2,128)} %exponents_in.1, s32[16,3072]{1,0:T(8,128)} %counts_in.1, s32[32]{0:T(128)} %tile_rows.1), custom_call_target="tpu_custom_call" | custom-call | flops 6442450944 | bytes 2097152 | tf_op jit(solution)/shard_map/pallas_call | solution.py:455
  72.2 1.7 %copy.6 = f32[16,32,64]{2,1,0:T(8,128)} copy(f32[16,32,64]{2,1,0:T(8,128)} %shard_map.46) | data formatting | bytes 262144

commit v4 on v3

--- a/solution.py
+++ b/solution.py
@@ -46,22 +46,23 @@
         largest = jnp.maximum(largest, jnp.max(jnp.abs(part), axis=0, keepdims=True))
     exponent = scale_exponent(largest)
     factor = jnp.exp2(15.0 - exponent)
-    for place, part in enumerate(parts):
-        dst[(*index, pl.ds(64 * place, 64))] = to_int16(part, factor)
-    tile = jnp.broadcast_to(exponent, (16, 128)).astype(jnp.int32).astype(jnp.int16)
-    dst[(*index, pl.ds(64 * len(parts), 16))] = tile
-
-
-def get_coded(src, index, place, count):
-    tile = src[(*index, pl.ds(64 * count, 16))].astype(jnp.int32).astype(F32)
+    dst[(*index, pl.ds(0, 16))] = jnp.broadcast_to(exponent, (16, 128)).astype(jnp.int32).astype(jnp.int16)
+    row = 16
+    for part in parts:
+        dst[(*index, pl.ds(row, part.shape[0]))] = to_int16(part, factor)
+        row += part.shape[0]
+
+
+def get_coded(src, index, place=0):
+    tile = src[(*index, pl.ds(0, 16))].astype(jnp.int32).astype(F32)
     factor = jnp.exp2(tile[0:1] - 15.0)
-    return from_int16(src[(*index, pl.ds(64 * place, 64))], factor)
+    return from_int16(src[(*index, pl.ds(16 + 64 * place, 64))], factor)
 
 
 def kernel(coded_in, exponents_in, counts_in, tile_rows, out,
-           coded, exponents, counts, xl, yl, cb, acc1, acc2, peer1, peer2, u, q1, near, far, u2, q2, last, f_buf,
-           g_buf, r_buf, tiles, send_tiles, got,
-           known1, known2, known4, ins, gs, gr, ps, pr, s1s, s1r, s2s, s2r, x1s, x1r, x2s, x2r):
+           coded, exponents, counts, xl, yl, cb, acc1, acc2, peer1, peer2, u, q1, near, far, u2, q2, last, own, f_buf,
+           tiles, swapped, send_tiles, got,
+           known1, known2, known4, ins, gs, gr, ps, pr, s1s, s1r, s2s, s2r, x2s, x2r):
     w = lax.axis_index("wide")
     n = lax.axis_index("narrow")
     z, c = w // 2, w % 2
@@ -199,7 +200,6 @@
 
     start_all(own_copies(0))
     start_all(own_copies(1))
-    tell(known1, 1)
     inputs[2].wait()
     for k in range(units):
         for r in range(REPLICAS):
@@ -208,22 +208,22 @@
     wait_near(0)
     start_all(forward_copies(0))
     start_all(own_copies(2))
-    pl.semaphore_wait(known1, 2)
-    tell(known2, 2)
     wait_near(1)
     start_all(forward_copies(1))
-    pl.semaphore_wait(known2, 2)
-    tell(known4, 4)
     wait_far(0)
+    tell(known1, 1)
     first(0)
     wait_near(2)
     start_all(forward_copies(2))
-    pl.semaphore_wait(known4, 2)
     second_all(0)
+    pl.semaphore_wait(known1, 2)
+    tell(known2, 2)
     wait_far(1)
     first(1)
     second_all(1)
     wait_far(2)
+    pl.semaphore_wait(known2, 2)
+    tell(known4, 4)
 
     @pl.when(c == 1)
     def _():
@@ -285,90 +285,150 @@
                     copy.start()
 
     step = z // 4
-
-    def hop_copy(s, d):
+    place = jnp.where(c == 0, y, x)
+
+    def hop_copy(to, d, rows):
         i = lax.rem(step + d, 4)
-        return remote(q2.at[s, i], last.at[d - 1, s], s2s.at[d - 1, s], s2r.at[d - 1, s], zc(cls + 4 * i, c), n)
-
-    for s in range(SIDE):
-        @pl.when(live(s))
-        def _():
-            for copy in near_copies(s):
-                copy.wait_recv()
-            for half in range(2):
-                for place in range(2):
-                    i = 2 * half + place
-                    u2[s, i] = (
-                        (u[s, cls, i] + get_coded(near, (0, s, half), place, 2))
-                        + (get_coded(near, (1, s, half), place, 2) + get_coded(far, (half, s), place, 2))
-                    )
-            for d in (2, 1, 3):
-                i = lax.rem(step + d, 4)
-                put_coded(q2, (s, i), [u2[s, i]])
-                hop_copy(s, d).start()
-
-    for s in range(SIDE):
-        @pl.when(live(s))
-        def _():
-            total = u2[s, step]
-            for d in (1, 2, 3):
-                hop_copy(s, d).wait_recv()
-                total = total + get_coded(last, (d - 1, s), 0, 1)
-            f_buf[s] = total
-
-        @pl.when(jnp.logical_not(live(s)))
-        def _():
-            f_buf[s] = jnp.zeros((64, 128), F32)
+        narrow = jnp.where(c == 0, at(x, to), at(to, y))
+        return remote(q2.at[to, i, pl.ds(0, rows)], last.at[d, place, pl.ds(0, rows)],
+                      s2s.at[d, to], s2r.at[d, place], zc(cls + 4 * i, c), narrow)
+
+    def hop_arrival(src, d, rows):
+        spot = last.at[d, src, pl.ds(0, rows)]
+        return remote(spot, spot, s2s.at[d, src], s2r.at[d, src], other, n)
+
+    def sized(run):
+        for k in range(SIDE):
+            pl.when(x == k)(lambda: run(16 + 16 * (SIDE - k)))
+
+    def reduced(s):
+        for copy in near_copies(s):
+            copy.wait_recv()
+        for half in range(2):
+            for p in range(2):
+                i = 2 * half + p
+                u2[s, i] = (
+                    (u[s, cls, i] + get_coded(near, (0, s, half), p))
+                    + (get_coded(near, (1, s, half), p) + get_coded(far, (half, s), p))
+                )
+
+    def repacked(i, to):
+        parts = []
+        for x1 in reversed(range(SIDE)):
+            rows = [u2[x1, i, 8 * k:8 * k + 8, HALF * to:HALF * to + HALF] for k in range(8)]
+            parts.append(jnp.concatenate([joined(rows[:4]), joined(rows[4:])], axis=0))
+        return parts
 
     @pl.when(c == 0)
     def _():
-        for y1 in range(SIDE):
-            g_buf[y1] = jnp.concatenate([f_buf[x1, :, HALF * y1:HALF * y1 + HALF] for x1 in range(SIDE)], axis=1)
+        for s in range(SIDE):
+            pl.when(s >= x)(lambda: reduced(s))
+
+            @pl.when(s < x)
+            def _():
+                u2[s] = jnp.zeros((4, 64, 128), F32)
+
+        pl.semaphore_wait(known4, 2)
+        for d in (2, 1, 3, 0):
+            i = lax.rem(step + d, 4)
+            for to in range(SIDE):
+                parts = repacked(i, to)
+
+                def ship():
+                    put_coded(q2, (to, i), parts)
+                    sized(lambda rows: hop_copy(to, d, rows).start())
+
+                if d:
+                    ship()
+                else:
+                    pl.when(to != y)(ship)
+
+                    @pl.when(to == y)
+                    def _():
+                        own[...] = jnp.concatenate(parts, axis=0)
+        for src in range(SIDE):
+            for d in (0, 1, 3, 2):
+                def arrive():
+                    sized(lambda rows: hop_arrival(src, d, rows).wait_recv())
+                if d:
+                    arrive()
+                else:
+                    pl.when(src != y)(arrive)
+            total = jnp.where(src == y, own[...], get_coded(last, (0, src)))
+            for d in (1, 3, 2):
+                total = total + get_coded(last, (d, src))
+            f_buf[src] = total
+
+    @pl.when(c == 1)
+    def _():
+        pl.semaphore_wait(known4, 2)
+        for s in range(SIDE):
+            @pl.when(s <= x)
+            def _():
+                reduced(s)
+                for d in (2, 1, 3, 0):
+                    i = lax.rem(step + d, 4)
+
+                    def ship():
+                        put_coded(q2, (s, i), [u2[s, i]])
+                        hop_copy(s, d, 80).start()
+
+                    if d:
+                        ship()
+                    else:
+                        pl.when(s != x)(ship)
+
+                        @pl.when(s == x)
+                        def _():
+                            own[...] = u2[s, i]
+        for src in range(SIDE):
+            @pl.when(src >= x)
+            def _():
+                for d in (0, 1, 3, 2):
+                    if d:
+                        hop_arrival(src, d, 80).wait_recv()
+                    else:
+                        pl.when(src != x)(lambda: hop_arrival(src, d, 80).wait_recv())
+                total = jnp.where(src == x, own[...], get_coded(last, (0, src)))
+                for d in (1, 3, 2):
+                    total = total + get_coded(last, (d, src))
+                f_buf[src] = total
+
+            @pl.when(src < x)
+            def _():
+                f_buf[src] = jnp.zeros((64, 128), F32)
+
+    sub = lax.broadcasted_iota(jnp.int32, (8, 128), 0)
+    lane = lax.broadcasted_iota(jnp.int32, (8, 128), 1)
+    offset = sub + 8 * (lane // HALF) - lane % HALF - COLS * n - HALF * c
+
+    def put_tile(t, tile):
+        tiles[t] = jnp.where(offset + 32 * t >= 0, tile / TOTAL, 0.0)
+
+    @pl.when(c == 0)
+    def _():
+        for x1 in range(SIDE):
+            for y1 in range(SIDE):
+                for hh in range(2):
+                    put_tile(2 * (SIDE * x1 + y1) + hh, f_buf[y1, pl.ds(16 * (SIDE - 1 - x1) + 8 * hh, 8), :])
 
     @pl.when(c == 1)
     def _():
         for x1 in range(SIDE):
-            turned = [f_buf[x1, HALF * half:HALF * half + HALF, :].T for half in range(2)]
-            g_buf[x1] = jnp.concatenate([turned[y1 // 2][64 * (y1 % 2):64 * (y1 % 2) + 64] for y1 in range(SIDE)], axis=1)
-
-    place = jnp.where(c == 0, y, x)
-
-    def line_copy(d, core):
-        to = lax.rem(place + d, SIDE)
-        narrow = jnp.where(c == 0, at(x, to), at(to, y))
-        sem = 2 * d + core
-        return remote(g_buf.at[to], r_buf.at[c, place], x1s.at[sem], x1r.at[c, d], zc(z, core), narrow)
-
-    for d in (2, 1, 3):
-        for core in range(2):
-            line_copy(d, core).start()
-    for core in range(2):
-        @pl.when(c != core)
-        def _():
-            line_copy(0, core).start()
-    r_buf[c, place] = g_buf[place]
-    for kind in range(2):
-        here = y if kind == 0 else x
-        for d in range(SIDE):
-            def arrived():
-                spot = r_buf.at[kind, lax.rem(here - d + SIDE, SIDE)]
-                remote(spot, spot, x1s.at[0], x1r.at[kind, d], other, n).wait_recv()
-            if d == 0:
-                pl.when(c != kind)(arrived)
-            else:
-                arrived()
-
-    sub = lax.broadcasted_iota(jnp.int32, (8, 128), 0)
-    lane = lax.broadcasted_iota(jnp.int32, (8, 128), 1)
-    for kind in range(2):
-        offset = sub + 8 * (lane // HALF) - lane % HALF - COLS * n - HALF * kind
-        for q in range(SIDE):
-            for hh in range(2):
-                groups = [r_buf[kind, q, 32 * hh + 8 * k:32 * hh + 8 * k + 8, :] for k in range(4)]
-                for g in range(SIDE):
-                    t = 2 * (SIDE * g + q if kind == 0 else SIDE * q + g) + hh
-                    tile = jnp.concatenate([group[:, HALF * g:HALF * g + HALF] for group in groups], axis=1)
-                    tiles[t, 8 * kind:8 * kind + 8, :] = jnp.where(offset + 32 * t >= 0, tile / TOTAL, 0.0)
+            for half in range(2):
+                turned = f_buf[x1, HALF * half:HALF * half + HALF, :].T
+                for k in range(4):
+                    rows = [turned[32 * k + 8 * g:32 * k + 8 * g + 8] for g in range(4)]
+                    put_tile(2 * SIDE * x1 + 4 * half + k, joined(rows))
+
+    mine = pl.ds(pl.multiple_of(8 * c, 8), 8)
+    swap = remote(swapped, send_tiles.at[:, mine], ps.at[SIDE], pr.at[SIDE], other, n)
+    for to in range(NZ):
+        swapped[to] = tiles[tile_rows[2 * to + 1 - c]]
+    swap.start()
+    for to in range(NZ):
+        send_tiles[to, mine, :] = tiles[tile_rows[2 * to + c]]
+    swap.wait_recv()
 
     def tile_copy(d):
         to = lax.rem(z + d, NZ)
@@ -376,9 +436,8 @@
 
     for d in (8, 7, 9, 6, 10, 5, 11, 4, 12, 3, 13, 2, 14, 1, 15):
         to = lax.rem(z + d, NZ)
-        send_tiles[to] = tiles[tile_rows[2 * to + c]]
         tile_copy(d).start()
-    got[z] = tiles[tile_rows[w]]
+    got[z] = send_tiles[z]
 
     for kc in range(len(CHUNKS)):
         for copy in own_copies(kc) + forward_copies(kc):
@@ -393,15 +452,18 @@
         def _():
             for copy in near_copies(s):
                 copy.wait_send()
-            for d in (1, 2, 3):
-                hop_copy(s, d).wait_send()
-    for d in range(1, SIDE):
-        for core in range(2):
-            line_copy(d, core).wait_send()
-    for core in range(2):
-        @pl.when(c != core)
-        def _():
-            line_copy(0, core).wait_send()
+    for to in range(SIDE):
+        for d in range(4):
+            away = jnp.logical_or(d > 0, to != place)
+
+            @pl.when(jnp.logical_and(c == 0, away))
+            def _():
+                sized(lambda rows: hop_copy(to, d, rows).wait_send())
+
+            @pl.when(jnp.logical_and(jnp.logical_and(c == 1, to <= x), away))
+            def _():
+                hop_copy(to, d, 80).wait_send()
+    swap.wait_send()
 
     most = pl.ds(0, NZ - 1)
     every = remote(send_tiles.at[most], got.at[most], x2s, x2r, other, n)
@@ -436,20 +498,19 @@
         pltpu.VMEM((2, SIDE, 144, 128), i16),
         pltpu.VMEM((SIDE, 4, 64, 128), F32),
         pltpu.VMEM((SIDE, 4, 80, 128), i16),
-        pltpu.VMEM((3, SIDE, 80, 128), i16),
+        pltpu.VMEM((4, SIDE, 80, 128), i16),
+        pltpu.VMEM((64, 128), F32),
         pltpu.VMEM((SIDE, 64, 128), F32),
-        pltpu.VMEM((SIDE, 64, 128), F32),
-        pltpu.VMEM((2, SIDE, 64, 128), F32),
-        pltpu.VMEM((WIDE, 16, 128), F32),
+        pltpu.VMEM((WIDE, 8, 128), F32),
+        pltpu.VMEM((NZ, 8, 128), F32),
         pltpu.VMEM((NZ, 16, 128), F32),
         pltpu.VMEM((NZ, 16, 128), F32),
         pltpu.SemaphoreType.REGULAR, pltpu.SemaphoreType.REGULAR, pltpu.SemaphoreType.REGULAR,
         dma((3,)),
         dma((len(CHUNKS), 8)), dma((len(CHUNKS), 8)),
-        dma((SIDE,)), dma((SIDE,)),
+        dma((SIDE + 1,)), dma((SIDE + 1,)),
         dma((4, SIDE)), dma((4, SIDE)),
-        dma((3, SIDE)), dma((3, SIDE)),
-        dma((2 * SIDE,)), dma((2, SIDE)),
+        dma((4, SIDE)), dma((4, SIDE)),
         dma, dma,
     ]
     return pl.pallas_call(

time: 74 us -> 71.1 us (0.961); the launches traced: 73.8 us -> 70.1 us
  Pallas kernels: 72.2 us -> 68.4 us
    pallas_call x1, Pallas kernels: 72.2 us -> 68.4 us  [per_device(): pl.pallas_call(kernel, out_shape=jax.ShapeDtypeStruct((REPLICAS, 32, COLS...]
where the time goes in v4:
time: 71.1 us; the launch traced here: 70.1 us
  Pallas kernels  68.4 us (96%)
  local copies, waits for them, and re-layouts  1.67 us (2%)
    pallas_call x1, Pallas kernels, per_device(): pl.pallas_call(kernel, out_shape=jax.ShapeDtypeStruct((REPLICAS, 32, COLS...  68.4 us
    unnamed x1, local copies, waits for them, and re-layouts  1.67 us

profile of v4, /device:TPU:1, one launch (start us, length us, event | category | flops | bytes accessed | tf_op | source)
XLA Modules:
  0.0 70.1 jit_solution(8194817121987441217)
XLA Ops:
  0.0 68.4 %shard_map.46 = f32[16,32,64]{2,1,0:T(8,128)} custom-call(bf16[64,3072]{1,0:T(8,128)(2,1)} %coded_in.1, s32[2,3072]{1,0:T(2,128)} %exponents_in.1, s32[16,3072]{1,0:T(8,128)} %counts_in.1, s32[32]{0:T(128)} %tile_rows.1), custom_call_target="tpu_custom_call" | custom-call | flops 6442450944 | bytes 2097152 | tf_op jit(solution)/shard_map/pallas_call | solution.py:516
  68.4 1.7 %copy.6 = f32[16,32,64]{2,1,0:T(8,128)} copy(f32[16,32,64]{2,1,0:T(8,128)} %shard_map.46) | data formatting | bytes 262144

commit v5 on v4

--- a/solution.py
+++ b/solution.py
@@ -13,6 +13,7 @@
 COLS = 64
 HALF = 32
 REPLICAS = 16
+HOPS = (6, -6, 2, -2)
 TOTAL = 98304
 UNIT = 256
 CHUNKS = ((0, 5), (5, 5), (10, 2))
@@ -60,7 +61,7 @@
 
 
 def kernel(coded_in, exponents_in, counts_in, tile_rows, out,
-           coded, exponents, counts, xl, yl, cb, acc1, acc2, peer1, peer2, u, q1, near, far, u2, q2, last, own, f_buf,
+           coded, exponents, counts, xl, yl, cb, acc1, acc2, peer1, peer2, u, q1, near, far, u2, q2, last, f_buf,
            tiles, swapped, send_tiles, got,
            known1, known2, known4, ins, gs, gr, ps, pr, s1s, s1r, s2s, s2r, x2s, x2r):
     w = lax.axis_index("wide")
@@ -261,7 +262,7 @@
     def live(s):
         return jnp.logical_or(jnp.logical_and(c == 0, s >= x), jnp.logical_and(c == 1, s <= x))
 
-    cls = lax.rem(z, 4)
+    cls = lax.rem(z + 2, 4)
 
     def klass(d):
         return lax.rem(cls + d + 4, 4)
@@ -284,22 +285,26 @@
                 for copy in parts:
                     copy.start()
 
-    step = z // 4
     place = jnp.where(c == 0, y, x)
 
+    def index_of(d):
+        return lax.rem(z + HOPS[d] + NZ, NZ) // 4
+
     def hop_copy(to, d, rows):
-        i = lax.rem(step + d, 4)
+        i = index_of(d)
         narrow = jnp.where(c == 0, at(x, to), at(to, y))
         return remote(q2.at[to, i, pl.ds(0, rows)], last.at[d, place, pl.ds(0, rows)],
-                      s2s.at[d, to], s2r.at[d, place], zc(cls + 4 * i, c), narrow)
+                      s2s.at[d, to], s2r.at[d, place], zc(z + HOPS[d], c), narrow)
 
     def hop_arrival(src, d, rows):
         spot = last.at[d, src, pl.ds(0, rows)]
         return remote(spot, spot, s2s.at[d, src], s2r.at[d, src], other, n)
 
-    def sized(run):
+    def sized(short, run):
         for k in range(SIDE):
-            pl.when(x == k)(lambda: run(16 + 16 * (SIDE - k)))
+            pl.when(jnp.logical_and(x == k, jnp.logical_not(short)))(lambda: run(16 + 16 * (SIDE - k)))
+            if k < SIDE - 1:
+                pl.when(jnp.logical_and(x == k, short))(lambda: run(16 * (SIDE - k)))
 
     def reduced(s):
         for copy in near_copies(s):
@@ -312,6 +317,9 @@
                     + (get_coded(near, (1, s, half), p) + get_coded(far, (half, s), p))
                 )
 
+    def gathered(src):
+        return (get_coded(last, (0, src)) + get_coded(last, (1, src))) + (get_coded(last, (2, src)) + get_coded(last, (3, src)))
+
     def repacked(i, to):
         parts = []
         for x1 in reversed(range(SIDE)):
@@ -329,35 +337,14 @@
                 u2[s] = jnp.zeros((4, 64, 128), F32)
 
         pl.semaphore_wait(known4, 2)
-        for d in (2, 1, 3, 0):
-            i = lax.rem(step + d, 4)
+        for d in range(4):
             for to in range(SIDE):
-                parts = repacked(i, to)
-
-                def ship():
-                    put_coded(q2, (to, i), parts)
-                    sized(lambda rows: hop_copy(to, d, rows).start())
-
-                if d:
-                    ship()
-                else:
-                    pl.when(to != y)(ship)
-
-                    @pl.when(to == y)
-                    def _():
-                        own[...] = jnp.concatenate(parts, axis=0)
+                put_coded(q2, (to, index_of(d)), repacked(index_of(d), to))
+                sized(to > y, lambda rows: hop_copy(to, d, rows).start())
         for src in range(SIDE):
-            for d in (0, 1, 3, 2):
-                def arrive():
-                    sized(lambda rows: hop_arrival(src, d, rows).wait_recv())
-                if d:
-                    arrive()
-                else:
-                    pl.when(src != y)(arrive)
-            total = jnp.where(src == y, own[...], get_coded(last, (0, src)))
-            for d in (1, 3, 2):
-                total = total + get_coded(last, (d, src))
-            f_buf[src] = total
+            for d in reversed(range(4)):
+                sized(src < y, lambda rows: hop_arrival(src, d, rows).wait_recv())
+            f_buf[src] = gathered(src)
 
     @pl.when(c == 1)
     def _():
@@ -366,33 +353,15 @@
             @pl.when(s <= x)
             def _():
                 reduced(s)
-                for d in (2, 1, 3, 0):
-                    i = lax.rem(step + d, 4)
-
-                    def ship():
-                        put_coded(q2, (s, i), [u2[s, i]])
-                        hop_copy(s, d, 80).start()
-
-                    if d:
-                        ship()
-                    else:
-                        pl.when(s != x)(ship)
-
-                        @pl.when(s == x)
-                        def _():
-                            own[...] = u2[s, i]
+                for d in range(4):
+                    put_coded(q2, (s, index_of(d)), [u2[s, index_of(d)]])
+                    hop_copy(s, d, 80).start()
         for src in range(SIDE):
             @pl.when(src >= x)
             def _():
-                for d in (0, 1, 3, 2):
-                    if d:
-                        hop_arrival(src, d, 80).wait_recv()
-                    else:
-                        pl.when(src != x)(lambda: hop_arrival(src, d, 80).wait_recv())
-                total = jnp.where(src == x, own[...], get_coded(last, (0, src)))
-                for d in (1, 3, 2):
-                    total = total + get_coded(last, (d, src))
-                f_buf[src] = total
+                for d in reversed(range(4)):
+                    hop_arrival(src, d, 80).wait_recv()
+                f_buf[src] = gathered(src)
 
             @pl.when(src < x)
             def _():
@@ -454,13 +423,11 @@
                 copy.wait_send()
     for to in range(SIDE):
         for d in range(4):
-            away = jnp.logical_or(d > 0, to != place)
-
-            @pl.when(jnp.logical_and(c == 0, away))
-            def _():
-                sized(lambda rows: hop_copy(to, d, rows).wait_send())
-
-            @pl.when(jnp.logical_and(jnp.logical_and(c == 1, to <= x), away))
+            @pl.when(c == 0)
+            def _():
+                sized(to > y, lambda rows: hop_copy(to, d, rows).wait_send())
+
+            @pl.when(jnp.logical_and(c == 1, to <= x))
             def _():
                 hop_copy(to, d, 80).wait_send()
     swap.wait_send()
@@ -499,7 +466,6 @@
         pltpu.VMEM((SIDE, 4, 64, 128), F32),
         pltpu.VMEM((SIDE, 4, 80, 128), i16),
         pltpu.VMEM((4, SIDE, 80, 128), i16),
-        pltpu.VMEM((64, 128), F32),
         pltpu.VMEM((SIDE, 64, 128), F32),
         pltpu.VMEM((WIDE, 8, 128), F32),
         pltpu.VMEM((NZ, 8, 128), F32),

time: 71.1 us -> 70.4 us (level); the launches traced: 70.1 us -> 70.2 us
  no operation moved by 1% of the time
where the time goes in v5:
time: 70.4 us; the launch traced here: 70.2 us
  Pallas kernels  68.5 us (97%)
  local copies, waits for them, and re-layouts  1.67 us (2%)
    pallas_call x1, Pallas kernels, per_device(): pl.pallas_call(kernel, out_shape=jax.ShapeDtypeStruct((REPLICAS, 32, COLS...  68.5 us
    unnamed x1, local copies, waits for them, and re-layouts  1.67 us

profile of v5, /device:TPU:1, one launch (start us, length us, event | category | flops | bytes accessed | tf_op | source)
XLA Modules:
  0.0 70.2 jit_solution(5200272990036226453)
XLA Ops:
  0.0 68.5 %shard_map.46 = f32[16,32,64]{2,1,0:T(8,128)} custom-call(bf16[64,3072]{1,0:T(8,128)(2,1)} %coded_in.1, s32[2,3072]{1,0:T(2,128)} %exponents_in.1, s32[16,3072]{1,0:T(8,128)} %counts_in.1, s32[32]{0:T(128)} %tile_rows.1), custom_call_target="tpu_custom_call" | custom-call | flops 6442450944 | bytes 2097152 | tf_op jit(solution)/shard_map/pallas_call | solution.py:482
  68.5 1.7 %copy.6 = f32[16,32,64]{2,1,0:T(8,128)} copy(f32[16,32,64]{2,1,0:T(8,128)} %shard_map.46) | data formatting | bytes 262144

commit v6 on v5

--- a/solution.py
+++ b/solution.py
@@ -245,6 +245,29 @@
     def _():
         first(2)
 
+    def live(s):
+        return jnp.logical_or(jnp.logical_and(c == 0, s >= x), jnp.logical_and(c == 1, s <= x))
+
+    cls = lax.rem(z + 2, 4)
+
+    def klass(d):
+        return lax.rem(cls + d + 4, 4)
+
+    def near_copies(s):
+        return [
+            remote(q1.at[s, klass(1)], near.at[0, s], s1s.at[0, s], s1r.at[0, s], zc(z + 1, c), n),
+            remote(q1.at[s, klass(-1)], near.at[1, s], s1s.at[1, s], s1r.at[1, s], zc(z - 1, c), n),
+            remote(q1.at[s, klass(2), 0], far.at[0, s], s1s.at[2, s], s1r.at[2, s], zc(z + 2, c), n),
+            remote(q1.at[s, klass(2), 1], far.at[1, s], s1s.at[3, s], s1r.at[3, s], zc(z - 2, c), n),
+        ]
+
+    def send_near(s):
+        copies = near_copies(s)
+        for d, parts in ((2, copies[2:]), (1, copies[:1]), (-1, copies[1:2])):
+            for half in range(2):
+                put_coded(q1, (s, klass(d), half), [u[s, klass(d), 2 * half], u[s, klass(d), 2 * half + 1]])
+            start_all(parts)
+
     for kind in range(2):
         for s in range(SIDE):
             @pl.when(jnp.logical_and(c == kind, used(kind, s)))
@@ -258,32 +281,7 @@
                         for half in range(2):
                             place = (s, pl.ds(HALF * r, HALF), pl.ds(128 * half, 128))
                             u[s, r % 4, r // 4, 32 * half:32 * half + 32, :] = acc2[place] + peer2[place]
-
-    def live(s):
-        return jnp.logical_or(jnp.logical_and(c == 0, s >= x), jnp.logical_and(c == 1, s <= x))
-
-    cls = lax.rem(z + 2, 4)
-
-    def klass(d):
-        return lax.rem(cls + d + 4, 4)
-
-    def near_copies(s):
-        return [
-            remote(q1.at[s, klass(1)], near.at[0, s], s1s.at[0, s], s1r.at[0, s], zc(z + 1, c), n),
-            remote(q1.at[s, klass(-1)], near.at[1, s], s1s.at[1, s], s1r.at[1, s], zc(z - 1, c), n),
-            remote(q1.at[s, klass(2), 0], far.at[0, s], s1s.at[2, s], s1r.at[2, s], zc(z + 2, c), n),
-            remote(q1.at[s, klass(2), 1], far.at[1, s], s1s.at[3, s], s1r.at[3, s], zc(z - 2, c), n),
-        ]
-
-    for s in range(SIDE):
-        @pl.when(live(s))
-        def _():
-            copies = near_copies(s)
-            for d, parts in ((2, copies[2:]), (1, copies[:1]), (-1, copies[1:2])):
-                for half in range(2):
-                    put_coded(q1, (s, klass(d), half), [u[s, klass(d), 2 * half], u[s, klass(d), 2 * half + 1]])
-                for copy in parts:
-                    copy.start()
+                send_near(s)
 
     place = jnp.where(c == 0, y, x)
 

time: 70.4 us -> 69.6 us (0.989)
    pallas_call x1, Pallas kernels: 68.5 us -> 67.8 us  [per_device(): pl.pallas_call(kernel, out_shape=jax.ShapeDtypeStruct((REPLICAS, 32, COLS...]
where the time goes in v6:
time: 69.6 us; the launch traced here: 69.4 us
  Pallas kernels  67.8 us (97%)
  local copies, waits for them, and re-layouts  1.67 us (2%)
    pallas_call x1, Pallas kernels, per_device(): pl.pallas_call(kernel, out_shape=jax.ShapeDtypeStruct((REPLICAS, 32, COLS...  67.8 us
    unnamed x1, local copies, waits for them, and re-layouts  1.67 us

profile of v6, /device:TPU:1, one launch (start us, length us, event | category | flops | bytes accessed | tf_op | source)
XLA Modules:
  0.0 69.4 jit_solution(8443063251254251904)
XLA Ops:
  0.0 67.8 %shard_map.46 = f32[16,32,64]{2,1,0:T(8,128)} custom-call(bf16[64,3072]{1,0:T(8,128)(2,1)} %coded_in.1, s32[2,3072]{1,0:T(2,128)} %exponents_in.1, s32[16,3072]{1,0:T(8,128)} %counts_in.1, s32[32]{0:T(128)} %tile_rows.1), custom_call_target="tpu_custom_call" | custom-call | flops 6442450944 | bytes 2097152 | tf_op jit(solution)/shard_map/pallas_call | solution.py:480
  67.8 1.7 %copy.6 = f32[16,32,64]{2,1,0:T(8,128)} copy(f32[16,32,64]{2,1,0:T(8,128)} %shard_map.46) | data formatting | bytes 262144
